TPU v7x, 32 devices: a whole 2x2x4 slice. The times are simulated.
32 devices in a mesh: ha: 8 (over z, y), vert: 4 (over x, core).
Axes of the slice: x: 2, y: 2, z: 4, core: 2. Of those that a mesh axis runs over, the one named last changes fastest.
Arguments:
- rhs: float32 [256, 32, 256], P('vert', 'ha'), may hold values from -4 to 4
- guess: float32 [256, 32, 256], P('vert', 'ha'), may hold values from -6 to 6
- vertical_coupling: float32 [256, 32, 256], P('vert', 'ha'), may hold values from 5 to 2500
- lateral_coupling: float32 [256, 32, 256], P('vert', 'ha'), may hold values from 0.25 to 1
Outputs:
- smoothed: float32 [256, 32, 256], P('vert', 'ha')
- coarse_residual: float32 [128, 32, 256], P('vert', 'ha')
All inputs are finite; a program needn't handle non-finite values.
Results may differ from a plain program's by a relative error of at most 0.0007.
Values sent between devices are 32-bit elements; how exact they have to be, the bound alone decides.
A program may use at most 128 MiB of HBM per device.

v0:
```python
import functools

import jax
import jax.numpy as jnp
from jax import lax
from jax.experimental import pallas as pl
from jax.experimental.pallas import tpu as pltpu
from jax.sharding import PartitionSpec as P

SWEEPS = 2
MESH = pl.DeviceIdType.MESH
LANES = 128


def kernel(
    depth, width, rhs, guess, up, lat, out, coarse,
    inv, fwd, bwd, first_g, last_g, src, work, res,
    low_in, pack, halo, ends0, ends, coef, edge_out, edge_in,
    low_send, low_recv, halo_send, halo_recv, end_send, end_recv, edge_send, edge_recv,
):
    levels = rhs.shape[0]
    rows = 4
    half = levels // 2
    chunk = levels // 8
    ha, vert = lax.axis_index("ha"), lax.axis_index("vert")
    sub = lax.broadcasted_iota(jnp.int32, (8, LANES), 0)
    lane = lax.broadcasted_iota(jnp.int32, (8, LANES), 1)
    row = sub % rows
    red = (row + lane) % 2 == 0
    zero = jnp.zeros((8, LANES), jnp.float32)

    def roll(a, by, axis):
        by = by % a.shape[axis]
        return a if by == 0 else pltpu.roll(a, by, axis)

    peers = [lax.rem(vert + o, depth) for o in range(1, depth)]
    barrier = pltpu.get_barrier_semaphore()
    for peer in peers:
        pl.semaphore_signal(barrier, inc=1, device_id=(ha, peer), device_id_type=MESH)

    @pl.when(ha > 0)
    def _():
        pl.semaphore_signal(barrier, inc=1, device_id=(ha - 1, vert), device_id_type=MESH)

    @pl.when(ha < width - 1)
    def _():
        pl.semaphore_signal(barrier, inc=1, device_id=(ha + 1, vert), device_id_type=MESH)

    def packed(acc, low_part, high_part, t, colour):
        result = []
        for side, from_row in ((0, rows - 1), (1, 0)):
            odd = (from_row + colour) % 2
            both = jnp.where(
                (lane % 2 == odd)[None], low_part, roll(high_part, -1 if odd else 1, 2)
            )
            both = roll(both, t - from_row, 1)
            result.append(both if acc is None else jnp.where((row == t)[None], both, acc[side]))
        return result

    def halo_copy(event, side):
        target = ha + 1 if side == 0 else ha - 1
        return pltpu.make_async_remote_copy(
            src_ref=pack.at[event, side], dst_ref=halo.at[event, side],
            send_sem=halo_send.at[event, side], recv_sem=halo_recv.at[event, side],
            device_id=(target, vert), device_id_type=MESH,
        )

    def halo_start(event, acc):
        pack[event, 0] = acc[0]
        pack[event, 1] = acc[1]

        @pl.when(ha < width - 1)
        def _():
            halo_copy(event, 0).start()

        @pl.when(ha > 0)
        def _():
            halo_copy(event, 1).start()

    def halo_wait(event):
        @pl.when(ha > 0)
        def _():
            halo_copy(event, 0).wait_recv()

        @pl.when(ha < width - 1)
        def _():
            halo_copy(event, 1).wait_recv()

    def unpacked(event, colour, t):
        lows, highs = [], []
        for side, from_row, to_row in ((0, rows - 1, 0), (1, 0, rows - 1)):
            odd = (from_row + colour) % 2
            both = roll(halo[event, side], to_row - t, 1)
            lows.append(both)
            highs.append(roll(both, 1 if odd else -1, 2))
        below, above = (row == 0)[None], (row == rows - 1)[None]
        return [
            jnp.where(below, pair[0], jnp.where(above, pair[1], 0.0)) for pair in (lows, highs)
        ]

    def lateral_inner(v):
        left = roll(v, 1, 2)
        right = roll(v, -1, 2)
        left = jnp.where(
            (lane == 0)[None], jnp.where((sub < rows)[None], 0.0, roll(left, rows, 1)), left
        )
        right = jnp.where(
            (lane == LANES - 1)[None], jnp.where((sub < rows)[None], roll(right, rows, 1), 0.0),
            right,
        )
        below = jnp.where((row == 0)[None], 0.0, roll(v, 1, 1))
        above = jnp.where((row == rows - 1)[None], 0.0, roll(v, -1, 1))
        return left + right + below + above

    def part(t):
        return pl.ds(t * chunk, chunk)

    def end_copy(event, buffer, slot, peer):
        return pltpu.make_async_remote_copy(
            src_ref=buffer.at[slot], dst_ref=buffer.at[slot],
            send_sem=end_send.at[event, peer], recv_sem=end_recv.at[event, slot],
            device_id=(ha, peer), device_id_type=MESH,
        )

    def end_buffer(event):
        return ends0 if event == 0 else ends.at[event - 1]

    def low_copy():
        return pltpu.make_async_remote_copy(
            src_ref=up.at[levels - 1], dst_ref=low_in, send_sem=low_send, recv_sem=low_recv,
            device_id=(ha, vert + 1), device_id_type=MESH,
        )

    def edge_copy(side):
        target = vert + 1 if side == 0 else vert - 1
        return pltpu.make_async_remote_copy(
            src_ref=edge_out.at[side], dst_ref=edge_in.at[side],
            send_sem=edge_send.at[side], recv_sem=edge_recv.at[side],
            device_id=(ha, target), device_id_type=MESH,
        )

    @pl.when(ha == 0)
    def _():
        for event in range(2 * SWEEPS + 1):
            halo[event, 0] = jnp.zeros(halo.shape[2:], jnp.float32)

    @pl.when(ha == width - 1)
    def _():
        for event in range(2 * SWEEPS + 1):
            halo[event, 1] = jnp.zeros(halo.shape[2:], jnp.float32)

    @pl.when(vert == 0)
    def _():
        low_in[...] = zero
        edge_in[0] = zero

    @pl.when(vert == depth - 1)
    def _():
        edge_in[1] = zero

    acc = None
    for t in range(4):
        acc = packed(acc, guess[part(t)], guess[part(t + 4)], t, 1)

    greeted = (ha > 0).astype(jnp.int32) + (ha < width - 1).astype(jnp.int32)
    pl.semaphore_wait(barrier, depth - 1 + greeted)

    @pl.when(vert < depth - 1)
    def _():
        low_copy().start()

    halo_start(0, acc)

    def partial_source(field):
        def body(t, carry):
            at = pl.ds(pl.multiple_of(t * chunk, chunk), chunk)
            src[at] = rhs[at] + lat[at] * lateral_inner(field[at])
            return carry
        lax.fori_loop(0, 8, body, 0, unroll=True)

    partial_source(guess)

    @pl.when(vert > 0)
    def _():
        low_copy().wait_recv()

    low0 = low_in[...]
    top = levels - 1
    up_top = up[top]

    def eliminate(k, carry, start):
        piv_l, g_l, piv_u, g_u = carry
        j = top - k
        low_k = low0 if start else up[k - 1]
        up_k = up[k]
        inv_k = 1.0 / (4.0 * lat[k] + up_k + low_k - low_k * piv_l)
        piv_l = up_k * inv_k
        g_l = inv_k if start else low_k * inv_k * g_l
        inv[k] = inv_k
        fwd[k] = low_k * inv_k
        bwd[k] = piv_l
        first_g[k] = g_l
        low_j, up_j = up[j - 1], up[j]
        inv_j = 1.0 / (4.0 * lat[j] + up_j + low_j - up_j * piv_u)
        piv_u = low_j * inv_j
        g_u = inv_j if start else up_j * inv_j * g_u
        inv[j] = inv_j
        fwd[j] = up_j * inv_j
        bwd[j] = piv_u
        last_g[j] = g_u
        return piv_l, g_l, piv_u, g_u

    carry = eliminate(0, (zero, zero, zero, zero), True)
    carry = lax.fori_loop(1, half, lambda k, c: eliminate(k, c, False), carry, unroll=True)
    piv_l, g_l, piv_u, g_u = carry
    meet = 1.0 / (1.0 - piv_l * piv_u)
    fa = g_l * meet
    fb = piv_u * fa
    lb = g_u * meet
    la = piv_l * lb
    first_g[half - 1] = fa
    first_g[half] = fb
    last_g[half] = lb
    last_g[half - 1] = la

    def respond(i, carry):
        fa, la, fb, lb = carry
        k = half - 1 - i
        j = half + i
        bk, bj = bwd[k], bwd[j]
        fa = first_g[k] + bk * fa
        la = bk * la
        fb = bj * fb
        lb = last_g[j] + bj * lb
        first_g[k] = fa
        last_g[k] = la
        first_g[j] = fb
        last_g[j] = lb
        return fa, la, fb, lb

    fa, la, fb, lb = lax.fori_loop(1, half, respond, (fa, la, fb, lb), unroll=True)
    own = [low0 * fa, low0 * fb, up_top * la, up_top * lb]

    def interface_coefficients():
        table = [[ends0[e, 2 + i] for i in range(4)] for e in range(depth)]
        slope_b, slope_a = zero, zero
        below = [zero] * (2 * depth)
        above = [zero] * (2 * depth)
        for e in range(depth - 1):
            v_f, v_l, w_f, w_l = table[e]
            keep = (e < vert).astype(jnp.float32)
            ratio = v_l * slope_b / (1.0 - v_f * slope_b)
            gain = keep * (v_l + ratio * v_f) + (1.0 - keep)
            below = [gain * b if n < 2 * e else b for n, b in enumerate(below)]
            below[2 * e] = keep * ratio
            below[2 * e + 1] = jnp.full((8, LANES), keep)
            slope_b = keep * (w_l + ratio * w_f) + (1.0 - keep) * slope_b
        for e in range(depth - 1, 0, -1):
            v_f, v_l, w_f, w_l = table[e]
            keep = (e > vert).astype(jnp.float32)
            ratio = w_f * slope_a / (1.0 - w_l * slope_a)
            gain = keep * (w_f + ratio * w_l) + (1.0 - keep)
            above = [gain * a if n > 2 * e + 1 else a for n, a in enumerate(above)]
            above[2 * e] = jnp.full((8, LANES), keep)
            above[2 * e + 1] = keep * ratio
            slope_a = keep * (v_f + ratio * v_l) + (1.0 - keep) * slope_a
        v_f, v_l, w_f, w_l = own
        c_ss, c_tt = 1.0 - slope_b * v_f, 1.0 - slope_a * w_l
        c_st, c_ts = slope_b * w_f, slope_a * v_l
        scale = 1.0 / (c_ss * c_tt - c_st * c_ts)
        for n in range(2 * depth):
            mine = (vert == n // 2).astype(jnp.float32)
            r_b = below[n] + mine * slope_b if n % 2 == 0 else below[n]
            r_a = above[n] + mine * slope_a if n % 2 == 1 else above[n]
            coef[0, n] = low0 * scale * (r_b * c_tt + c_st * r_a)
            coef[1, n] = up_top * scale * (c_ss * r_a + c_ts * r_b)

    reach = {}
    for event in range(2 * SWEEPS):
        colour = event % 2
        chosen = red if colour == 0 else jnp.logical_not(red)
        halo_wait(event)
        dot_f, dot_l = zero, zero
        for t in range(4):
            for where, outer in zip((part(t), part(t + 4)), unpacked(event, 1 - colour, t)):
                full = src[where] + lat[where] * outer
                src[where] = full
                dot_f = dot_f + jnp.sum(full * first_g[where], axis=0)
                dot_l = dot_l + jnp.sum(full * last_g[where], axis=0)
        buffer = end_buffer(event)
        buffer[vert, 0] = dot_f
        buffer[vert, 1] = dot_l
        if event == 0:
            for i in range(4):
                buffer[vert, 2 + i] = own[i]
        for peer in peers:
            end_copy(event, buffer, vert, peer).start()

        def forward(k, carry):
            f_l, f_u = carry
            j = top - k
            f_l = src[k] * inv[k] + fwd[k] * f_l
            f_u = src[j] * inv[j] + fwd[j] * f_u
            work[k] = f_l
            work[j] = f_u
            return f_l, f_u

        f_l, f_u = lax.fori_loop(0, half, forward, (zero, zero), unroll=True)
        y_l = (f_l + piv_l * f_u) * meet
        y_u = f_u + piv_u * y_l
        work[half - 1] = y_l
        work[half] = y_u

        def backward(i, carry):
            y_l, y_u = carry
            k = half - 1 - i
            j = half + i
            y_l = work[k] + bwd[k] * y_l
            y_u = work[j] + bwd[j] * y_u
            work[k] = y_l
            work[j] = y_u
            return y_l, y_u

        lax.fori_loop(1, half, backward, (y_l, y_u), unroll=True)
        for peer in peers:
            end_copy(event, buffer, peer, peer).wait_recv()
        if event == 0:
            interface_coefficients()
        from_b, from_a = zero, zero
        for n in range(2 * depth):
            value = buffer[n // 2, n % 2]
            from_b = from_b + coef[0, n] * value
            from_a = from_a + coef[1, n] * value
        reach[colour] = (from_b, from_a)
        old = guess if event == 0 else out
        acc = None
        for t in range(4):
            pair = []
            for where in (part(t), part(t + 4)):
                new = work[where] + first_g[where] * from_b + last_g[where] * from_a
                new = jnp.where(chosen[None], new, old[where])
                out[where] = new
                pair.append(new)
            acc = packed(acc, pair[0], pair[1], t, colour)
        halo_start(event + 1, acc)
        if event == 2 * SWEEPS - 1:
            def keep_source(t, carry):
                at = pl.ds(pl.multiple_of(t * chunk, chunk), chunk)
                inner = rhs[at] + lat[at] * lateral_inner(out[at])
                src[at] = jnp.where(red[None], inner, src[at])
                return carry
            lax.fori_loop(0, 8, keep_source, 0, unroll=True)
        else:
            partial_source(out)

    from_b = jnp.where(red, reach[0][0], reach[1][0])
    from_a = jnp.where(red, reach[0][1], reach[1][1])

    def applied(k):
        low_k = low0 if k == 0 else up[k - 1]
        under = from_b if k == 0 else low_k * out[k - 1]
        over = from_a if k == top else up[k] * out[k + 1]
        return (4.0 * lat[k] + up[k] + low_k) * out[k] - over - under

    res[0] = src[0] - applied(0)
    res[top] = src[top] - applied(top)

    def inner_level(k, carry):
        low_k, up_k = up[k - 1], up[k]
        res[k] = src[k] - (
            (4.0 * lat[k] + up_k + low_k) * out[k] - up_k * out[k + 1] - low_k * out[k - 1]
        )
        return carry

    lax.fori_loop(1, top, inner_level, 0, unroll=True)
    halo_wait(2 * SWEEPS)
    for t in range(4):
        for where, outer in zip((part(t), part(t + 4)), unpacked(2 * SWEEPS, 1, t)):
            res[where] = res[where] + lat[where] * jnp.where(red[None], outer, 0.0)
    edge_out[0] = res[top]
    edge_out[1] = res[0]

    @pl.when(vert < depth - 1)
    def _():
        edge_copy(0).start()

    @pl.when(vert > 0)
    def _():
        edge_copy(1).start()

    def restrict(m, carry):
        coarse[m] = (
            res[2 * m - 1] + 3.0 * res[2 * m] + 3.0 * res[2 * m + 1] + res[2 * m + 2]
        ) * 0.125
        return carry

    last = levels // 2 - 1
    lax.fori_loop(1, last, restrict, 0, unroll=True)

    @pl.when(vert > 0)
    def _():
        edge_copy(0).wait_recv()

    @pl.when(vert < depth - 1)
    def _():
        edge_copy(1).wait_recv()

    coarse[0] = (edge_in[0] + 3.0 * res[0] + 3.0 * res[1] + res[2]) * 0.125
    coarse[last] = (res[top - 2] + 3.0 * res[top - 1] + 3.0 * res[top] + edge_in[1]) * 0.125

    @pl.when(vert < depth - 1)
    def _():
        low_copy().wait_send()
        edge_copy(0).wait_send()

    @pl.when(vert > 0)
    def _():
        edge_copy(1).wait_send()

    for event in range(2 * SWEEPS):
        for peer in peers:
            end_copy(event, end_buffer(event), vert, peer).wait_send()
    for event in range(2 * SWEEPS + 1):
        @pl.when(ha < width - 1)
        def _():
            halo_copy(event, 0).wait_send()

        @pl.when(ha > 0)
        def _():
            halo_copy(event, 1).wait_send()


def to_tiles(a):
    levels, rows, cols = a.shape
    return a.reshape(levels, rows, cols // LANES, LANES).transpose(0, 2, 1, 3).reshape(
        levels, rows * (cols // LANES), LANES
    )


def from_tiles(a, rows, cols):
    levels = a.shape[0]
    return a.reshape(levels, cols // LANES, rows, LANES).transpose(0, 2, 1, 3).reshape(
        levels, rows, cols
    )


def local(depth, width, rhs, guess, vertical_coupling, lateral_coupling):
    levels, rows, cols = guess.shape
    f32 = jnp.float32
    tile = (8, LANES)
    field = pltpu.VMEM((levels,) + tile, f32)
    events = 2 * SWEEPS + 1
    dma = pltpu.SemaphoreType.DMA
    vmem = pl.BlockSpec(memory_space=pltpu.VMEM)
    smoothed, coarse = pl.pallas_call(
        functools.partial(kernel, depth, width),
        out_shape=(
            jax.ShapeDtypeStruct((levels,) + tile, f32),
            jax.ShapeDtypeStruct((levels // 2,) + tile, f32),
        ),
        in_specs=[vmem] * 4,
        out_specs=(vmem, vmem),
        scratch_shapes=[field] * 8 + [
            pltpu.VMEM(tile, f32),
            pltpu.VMEM((events, 2, levels // 8) + tile, f32),
            pltpu.VMEM((events, 2, levels // 8) + tile, f32),
            pltpu.VMEM((depth, 6) + tile, f32),
            pltpu.VMEM((events - 2, depth, 2) + tile, f32),
            pltpu.VMEM((2, 2 * depth) + tile, f32),
            pltpu.VMEM((2,) + tile, f32),
            pltpu.VMEM((2,) + tile, f32),
            dma, dma,
            dma((events, 2)), dma((events, 2)),
            dma((events - 1, depth)), dma((events - 1, depth)),
            dma((2,)), dma((2,)),
        ],
        compiler_params=pltpu.CompilerParams(
            collective_id=0, has_side_effects=True, vmem_limit_bytes=32 * 1024 * 1024
        ),
        cost_estimate=pl.CostEstimate(
            flops=200 * levels * rows * cols, bytes_accessed=22 * levels * rows * cols,
            transcendentals=0,
        ),
    )(*[to_tiles(a) for a in (rhs, guess, vertical_coupling, lateral_coupling)])
    return from_tiles(smoothed, rows, cols), from_tiles(coarse, rows, cols)


def solution(mesh):
    spec = P("vert", "ha", None)
    return jax.shard_map(
        functools.partial(local, mesh.shape["vert"], mesh.shape["ha"]),
        mesh=mesh,
        in_specs=(spec,) * 4,
        out_specs=(spec, spec),
        check_vma=False,
    )
```

profile of v0, /device:TPU:1, one launch (start us, length us, event | category | flops | bytes accessed | tf_op | source)
XLA Modules:
  0.0 41.5 jit_solution(9570238498867198311)
XLA Ops:
  0.6 0.0 copy-start
  0.6 0.9 %copy-done = f32[64,4,256]{2,1,0:T(4,128)S(1)} copy-done((f32[64,4,256]{2,1,0:T(4,128)S(1)}, f32[64,4,256]{2,1,0:T(4,128)}, u32[]{:S(2)}) %copy-start) | copy-done | bytes 262168
  1.6 0.0 copy-start.1
  1.6 0.9 %copy-done.1 = f32[64,4,256]{2,1,0:T(4,128)S(1)} copy-done((f32[64,4,256]{2,1,0:T(4,128)S(1)}, f32[64,4,256]{2,1,0:T(4,128)}, u32[]{:S(2)}) %copy-start.1) | copy-done | bytes 262168
  2.5 0.0 copy-start.2
  2.5 0.9 %copy-done.2 = f32[64,4,256]{2,1,0:T(4,128)S(1)} copy-done((f32[64,4,256]{2,1,0:T(4,128)S(1)}, f32[64,4,256]{2,1,0:T(4,128)}, u32[]{:S(2)}) %copy-start.2) | copy-done | bytes 262168
  3.5 0.0 copy-start.3
  3.5 0.9 %copy-done.3 = f32[64,4,256]{2,1,0:T(4,128)S(1)} copy-done((f32[64,4,256]{2,1,0:T(4,128)S(1)}, f32[64,4,256]{2,1,0:T(4,128)}, u32[]{:S(2)}) %copy-start.3) | copy-done | bytes 262168
  4.4 35.7 %shard_map.59 = (f32[64,8,128]{2,1,0:T(8,128)S(1)}, f32[32,8,128]{2,1,0:T(8,128)S(1)}) custom-call(f32[64,8,128]{2,1,0:T(8,128)S(1)} %bitcast.31, f32[64,8,128]{2,1,0:T(8,128)S(1)} %bitcast.32, f32[64,8,128]{2,1,0:T(8,128)S(1)} %bitcast.33, f32[64,8,128]{2,1,0:T(8,128)S(1)} %bitcast.34), custom_call_target="tpu_custom_call" | custom-call | flops 13107200 | bytes 1441792 | tf_op jit(solution)/shard_map/pallas_call | solution.py:455
  40.1 0.7 %copy.14 = f32[64,4,256]{2,1,0:T(4,128)} copy(f32[64,4,256]{2,1,0:T(4,128)S(1)} %bitcast.30) | data formatting | bytes 524288
  40.8 0.7 %copy.15 = f32[32,4,256]{2,1,0:T(4,128)} copy(f32[32,4,256]{2,1,0:T(4,128)S(1)} %bitcast.35) | data formatting | bytes 262144
Async XLA Ops:
  0.6 1.0 %copy-start = (f32[64,4,256]{2,1,0:T(4,128)S(1)}, f32[64,4,256]{2,1,0:T(4,128)}, u32[]{:S(2)}) copy-start(f32[64,4,256]{2,1,0:T(4,128)} %param.4) | copy-start | bytes 786436
  1.6 0.9 %copy-start.1 = (f32[64,4,256]{2,1,0:T(4,128)S(1)}, f32[64,4,256]{2,1,0:T(4,128)}, u32[]{:S(2)}) copy-start(f32[64,4,256]{2,1,0:T(4,128)} %param.5) | copy-start | bytes 786436
  2.5 0.9 %copy-start.2 = (f32[64,4,256]{2,1,0:T(4,128)S(1)}, f32[64,4,256]{2,1,0:T(4,128)}, u32[]{:S(2)}) copy-start(f32[64,4,256]{2,1,0:T(4,128)} %param.6) | copy-start | bytes 786436
  3.5 0.9 %copy-start.3 = (f32[64,4,256]{2,1,0:T(4,128)S(1)}, f32[64,4,256]{2,1,0:T(4,128)}, u32[]{:S(2)}) copy-start(f32[64,4,256]{2,1,0:T(4,128)} %param.7) | copy-start | bytes 786436
where the time goes:
time: 41.7 us; the launch traced here: 41.5 us
  Pallas kernels  35.7 us (86%)
  local copies, waits for them, and re-layouts  5.15 us (12%)
  between operations  0.65 us (2%)
    pallas_call x1, Pallas kernels, local(): pl.pallas_call(functools.partial(kernel, depth, width), out_shape=(jax.Sh...  35.7 us
    unnamed x10, local copies, waits for them, and re-layouts  5.15 us

commit v1 on v0

--- a/solution.py
+++ b/solution.py
@@ -13,12 +13,15 @@
 
 
 def kernel(
-    depth, width, rhs, guess, up, lat, out, coarse,
+    depth, width, rhs_hbm, guess_hbm, up_hbm, lat_hbm, out, coarse,
+    rhs, guess, up, lat,
     inv, fwd, bwd, first_g, last_g, src, work, res,
     low_in, pack, halo, ends0, ends, coef, edge_out, edge_in,
+    row0_out, row0_in, row_out, row_in, row_coef, unit_pack, unit_halo, joined,
     low_send, low_recv, halo_send, halo_recv, end_send, end_recv, edge_send, edge_recv,
+    load_sem, row_send, row_recv, unit_send, unit_recv,
 ):
-    levels = rhs.shape[0]
+    levels = rhs_hbm.shape[0]
     rows = 4
     half = levels // 2
     chunk = levels // 8
@@ -33,18 +36,31 @@
         by = by % a.shape[axis]
         return a if by == 0 else pltpu.roll(a, by, axis)
 
+    loads = [
+        pltpu.make_async_copy(source, target, load_sem.at[i])
+        for i, (source, target) in enumerate(
+            ((guess_hbm, guess), (up_hbm, up), (lat_hbm, lat), (rhs_hbm, rhs))
+        )
+    ]
+    for load in loads:
+        load.start()
+
     peers = [lax.rem(vert + o, depth) for o in range(1, depth)]
     barrier = pltpu.get_barrier_semaphore()
     for peer in peers:
         pl.semaphore_signal(barrier, inc=1, device_id=(ha, peer), device_id_type=MESH)
 
+    everyone = [lax.rem(vert + o, depth) for o in range(depth)]
+
     @pl.when(ha > 0)
     def _():
-        pl.semaphore_signal(barrier, inc=1, device_id=(ha - 1, vert), device_id_type=MESH)
+        for peer in everyone:
+            pl.semaphore_signal(barrier, inc=1, device_id=(ha - 1, peer), device_id_type=MESH)
 
     @pl.when(ha < width - 1)
     def _():
-        pl.semaphore_signal(barrier, inc=1, device_id=(ha + 1, vert), device_id_type=MESH)
+        for peer in everyone:
+            pl.semaphore_signal(barrier, inc=1, device_id=(ha + 1, peer), device_id_type=MESH)
 
     def packed(acc, low_part, high_part, t, colour):
         result = []
@@ -86,11 +102,11 @@
         def _():
             halo_copy(event, 1).wait_recv()
 
-    def unpacked(event, colour, t):
+    def unpacked(planes, colour, t):
         lows, highs = [], []
         for side, from_row, to_row in ((0, rows - 1, 0), (1, 0, rows - 1)):
             odd = (from_row + colour) % 2
-            both = roll(halo[event, side], to_row - t, 1)
+            both = roll(planes[side], to_row - t, 1)
             lows.append(both)
             highs.append(roll(both, 1 if odd else -1, 2))
         below, above = (row == 0)[None], (row == rows - 1)[None]
@@ -125,6 +141,98 @@
     def end_buffer(event):
         return ends0 if event == 0 else ends.at[event - 1]
 
+    def row_buffers(event):
+        return (row0_out, row0_in) if event == 0 else (row_out.at[event - 1], row_in.at[event - 1])
+
+    def row_copy(event, side, slot, peer):
+        source, target = row_buffers(event)
+        return pltpu.make_async_remote_copy(
+            src_ref=source.at[side], dst_ref=target.at[side, slot],
+            send_sem=row_send.at[event, side, peer], recv_sem=row_recv.at[event, side, slot],
+            device_id=(ha + 1 if side == 0 else ha - 1, peer), device_id_type=MESH,
+        )
+
+    def unit_copy(colour, side):
+        return pltpu.make_async_remote_copy(
+            src_ref=unit_pack.at[colour, side], dst_ref=unit_halo.at[colour, side],
+            send_sem=unit_send.at[colour, side], recv_sem=unit_recv.at[colour, side],
+            device_id=(ha + 1 if side == 0 else ha - 1, vert), device_id_type=MESH,
+        )
+
+    def to_sides(act):
+        @pl.when(ha < width - 1)
+        def _():
+            act(0)
+
+        @pl.when(ha > 0)
+        def _():
+            act(1)
+
+    def from_sides(act):
+        @pl.when(ha > 0)
+        def _():
+            act(0)
+
+        @pl.when(ha < width - 1)
+        def _():
+            act(1)
+
+    def rows_start(event, items):
+        source, _ = row_buffers(event)
+        for side, from_row in ((0, rows - 1), (1, 0)):
+            for first in range(0, len(items), rows):
+                tile = zero
+                for t, item in enumerate(items[first:first + rows]):
+                    tile = jnp.where(row == t, roll(item, t - from_row, 0), tile)
+                source[side, first // rows] = tile
+
+        def start(side):
+            for peer in everyone:
+                row_copy(event, side, vert, peer).start()
+
+        to_sides(start)
+
+    def rows_wait(event):
+        def wait(side):
+            for peer in everyone:
+                row_copy(event, side, peer, peer).wait_recv()
+
+        from_sides(wait)
+
+    def row_item(event, slot, item):
+        _, target = row_buffers(event)
+        t = item % rows
+        return jnp.where(
+            row == 0, roll(target[0, slot, item // rows], -t, 0),
+            jnp.where(row == rows - 1, roll(target[1, slot, item // rows], rows - 1 - t, 0), 0.0),
+        )
+
+    def units_start(colour):
+        for i, field in enumerate((first_g, last_g)):
+            acc = None
+            for t in range(4):
+                acc = packed(acc, field[part(t)], field[part(t + 4)], t, colour)
+            unit_pack[colour, 0, i] = acc[0]
+            unit_pack[colour, 1, i] = acc[1]
+        to_sides(lambda side: unit_copy(colour, side).start())
+
+    def spread(value, side, colour):
+        sign = 1 if side == 0 else -1
+        kept = jnp.where(row == (0 if side == 0 else rows - 1), value, 0.0)
+        total = kept
+        for by in range(1, rows):
+            total = total + roll(kept, sign * by, 0)
+        odd = ((rows - 1 if side == 0 else 0) + colour) % 2
+        return jnp.where(lane % 2 == odd, total, roll(total, -1 if odd else 1, 1))
+
+    def join_planes(event, colour, from_b, from_a):
+        for side in range(2):
+            b = spread(from_b, side, colour)
+            a = spread(from_a, side, colour)
+            joined[side] = (
+                halo[event, side] + unit_halo[colour, side, 0] * b + unit_halo[colour, side, 1] * a
+            )
+
     def low_copy():
         return pltpu.make_async_remote_copy(
             src_ref=up.at[levels - 1], dst_ref=low_in, send_sem=low_send, recv_sem=low_recv,
@@ -143,11 +251,21 @@
     def _():
         for event in range(2 * SWEEPS + 1):
             halo[event, 0] = jnp.zeros(halo.shape[2:], jnp.float32)
+        for colour in range(2):
+            unit_halo[colour, 0] = jnp.zeros(unit_halo.shape[2:], jnp.float32)
+        row0_in[0] = jnp.zeros(row0_in.shape[1:], jnp.float32)
+        for event in range(2 * SWEEPS - 1):
+            row_in[event, 0] = jnp.zeros(row_in.shape[2:], jnp.float32)
 
     @pl.when(ha == width - 1)
     def _():
         for event in range(2 * SWEEPS + 1):
             halo[event, 1] = jnp.zeros(halo.shape[2:], jnp.float32)
+        for colour in range(2):
+            unit_halo[colour, 1] = jnp.zeros(unit_halo.shape[2:], jnp.float32)
+        row0_in[1] = jnp.zeros(row0_in.shape[1:], jnp.float32)
+        for event in range(2 * SWEEPS - 1):
+            row_in[event, 1] = jnp.zeros(row_in.shape[2:], jnp.float32)
 
     @pl.when(vert == 0)
     def _():
@@ -158,18 +276,23 @@
     def _():
         edge_in[1] = zero
 
+    loads[0].wait()
     acc = None
     for t in range(4):
         acc = packed(acc, guess[part(t)], guess[part(t + 4)], t, 1)
 
     greeted = (ha > 0).astype(jnp.int32) + (ha < width - 1).astype(jnp.int32)
-    pl.semaphore_wait(barrier, depth - 1 + greeted)
+    pl.semaphore_wait(barrier, depth - 1 + depth * greeted)
+
+    loads[1].wait()
 
     @pl.when(vert < depth - 1)
     def _():
         low_copy().start()
 
     halo_start(0, acc)
+    loads[2].wait()
+    loads[3].wait()
 
     def partial_source(field):
         def body(t, carry):
@@ -241,8 +364,7 @@
     fa, la, fb, lb = lax.fori_loop(1, half, respond, (fa, la, fb, lb), unroll=True)
     own = [low0 * fa, low0 * fb, up_top * la, up_top * lb]
 
-    def interface_coefficients():
-        table = [[ends0[e, 2 + i] for i in range(4)] for e in range(depth)]
+    def interface_coefficients(table, own, low0, up_top, coef):
         slope_b, slope_a = zero, zero
         below = [zero] * (2 * depth)
         above = [zero] * (2 * depth)
@@ -276,13 +398,15 @@
             coef[1, n] = up_top * scale * (c_ss * r_a + c_ts * r_b)
 
     reach = {}
+    planes = halo.at[0]
     for event in range(2 * SWEEPS):
         colour = event % 2
         chosen = red if colour == 0 else jnp.logical_not(red)
-        halo_wait(event)
+        if event == 0:
+            halo_wait(0)
         dot_f, dot_l = zero, zero
         for t in range(4):
-            for where, outer in zip((part(t), part(t + 4)), unpacked(event, 1 - colour, t)):
+            for where, outer in zip((part(t), part(t + 4)), unpacked(planes, 1 - colour, t)):
                 full = src[where] + lat[where] * outer
                 src[where] = full
                 dot_f = dot_f + jnp.sum(full * first_g[where], axis=0)
@@ -293,8 +417,11 @@
         if event == 0:
             for i in range(4):
                 buffer[vert, 2 + i] = own[i]
+        rows_start(event, [dot_f, dot_l] + (own + [low0, up_top] if event == 0 else []))
         for peer in peers:
             end_copy(event, buffer, vert, peer).start()
+        if event == 0:
+            units_start(0)
 
         def forward(k, carry):
             f_l, f_u = carry
@@ -322,10 +449,17 @@
             return y_l, y_u
 
         lax.fori_loop(1, half, backward, (y_l, y_u), unroll=True)
+        acc = None
+        for t in range(4):
+            acc = packed(acc, work[part(t)], work[part(t + 4)], t, colour)
+        halo_start(event + 1, acc)
+        if event == 0:
+            units_start(1)
         for peer in peers:
             end_copy(event, buffer, peer, peer).wait_recv()
         if event == 0:
-            interface_coefficients()
+            table = [[ends0[e, 2 + i] for i in range(4)] for e in range(depth)]
+            interface_coefficients(table, own, low0, up_top, coef)
         from_b, from_a = zero, zero
         for n in range(2 * depth):
             value = buffer[n // 2, n % 2]
@@ -333,16 +467,10 @@
             from_a = from_a + coef[1, n] * value
         reach[colour] = (from_b, from_a)
         old = guess if event == 0 else out
-        acc = None
-        for t in range(4):
-            pair = []
-            for where in (part(t), part(t + 4)):
-                new = work[where] + first_g[where] * from_b + last_g[where] * from_a
-                new = jnp.where(chosen[None], new, old[where])
-                out[where] = new
-                pair.append(new)
-            acc = packed(acc, pair[0], pair[1], t, colour)
-        halo_start(event + 1, acc)
+        for t in range(8):
+            where = part(t)
+            new = work[where] + first_g[where] * from_b + last_g[where] * from_a
+            out[where] = jnp.where(chosen[None], new, old[where])
         if event == 2 * SWEEPS - 1:
             def keep_source(t, carry):
                 at = pl.ds(pl.multiple_of(t * chunk, chunk), chunk)
@@ -352,6 +480,21 @@
             lax.fori_loop(0, 8, keep_source, 0, unroll=True)
         else:
             partial_source(out)
+        rows_wait(event)
+        if event == 0:
+            table = [[row_item(0, e, 2 + i) for i in range(4)] for e in range(depth)]
+            mine = [row_item(0, vert, 2 + i) for i in range(6)]
+            interface_coefficients(table, mine[:4], mine[4], mine[5], row_coef)
+        from_b, from_a = zero, zero
+        for n in range(2 * depth):
+            value = row_item(event, n // 2, n % 2)
+            from_b = from_b + row_coef[0, n] * value
+            from_a = from_a + row_coef[1, n] * value
+        if event < 2:
+            from_sides(lambda side: unit_copy(colour, side).wait_recv())
+        halo_wait(event + 1)
+        join_planes(event + 1, colour, from_b, from_a)
+        planes = joined
 
     from_b = jnp.where(red, reach[0][0], reach[1][0])
     from_a = jnp.where(red, reach[0][1], reach[1][1])
@@ -362,8 +505,23 @@
         over = from_a if k == top else up[k] * out[k + 1]
         return (4.0 * lat[k] + up[k] + low_k) * out[k] - over - under
 
-    res[0] = src[0] - applied(0)
-    res[top] = src[top] - applied(top)
+    for t in range(4):
+        for where, outer in zip((part(t), part(t + 4)), unpacked(joined, 1, t)):
+            src[where] = src[where] + lat[where] * jnp.where(red[None], outer, 0.0)
+    bottom_res = src[0] - applied(0)
+    top_res = src[top] - applied(top)
+    res[0] = bottom_res
+    res[top] = top_res
+    edge_out[0] = top_res
+    edge_out[1] = bottom_res
+
+    @pl.when(vert < depth - 1)
+    def _():
+        edge_copy(0).start()
+
+    @pl.when(vert > 0)
+    def _():
+        edge_copy(1).start()
 
     def inner_level(k, carry):
         low_k, up_k = up[k - 1], up[k]
@@ -373,20 +531,6 @@
         return carry
 
     lax.fori_loop(1, top, inner_level, 0, unroll=True)
-    halo_wait(2 * SWEEPS)
-    for t in range(4):
-        for where, outer in zip((part(t), part(t + 4)), unpacked(2 * SWEEPS, 1, t)):
-            res[where] = res[where] + lat[where] * jnp.where(red[None], outer, 0.0)
-    edge_out[0] = res[top]
-    edge_out[1] = res[0]
-
-    @pl.when(vert < depth - 1)
-    def _():
-        edge_copy(0).start()
-
-    @pl.when(vert > 0)
-    def _():
-        edge_copy(1).start()
 
     def restrict(m, carry):
         coarse[m] = (
@@ -420,6 +564,14 @@
     for event in range(2 * SWEEPS):
         for peer in peers:
             end_copy(event, end_buffer(event), vert, peer).wait_send()
+
+        def sent(side):
+            for peer in everyone:
+                row_copy(event, side, vert, peer).wait_send()
+
+        to_sides(sent)
+    for colour in range(2):
+        to_sides(lambda side: unit_copy(colour, side).wait_send())
     for event in range(2 * SWEEPS + 1):
         @pl.when(ha < width - 1)
         def _():
@@ -458,9 +610,9 @@
             jax.ShapeDtypeStruct((levels,) + tile, f32),
             jax.ShapeDtypeStruct((levels // 2,) + tile, f32),
         ),
-        in_specs=[vmem] * 4,
+        in_specs=[pl.BlockSpec(memory_space=pl.ANY)] * 4,
         out_specs=(vmem, vmem),
-        scratch_shapes=[field] * 8 + [
+        scratch_shapes=[field] * 12 + [
             pltpu.VMEM(tile, f32),
             pltpu.VMEM((events, 2, levels // 8) + tile, f32),
             pltpu.VMEM((events, 2, levels // 8) + tile, f32),
@@ -469,13 +621,22 @@
             pltpu.VMEM((2, 2 * depth) + tile, f32),
             pltpu.VMEM((2,) + tile, f32),
             pltpu.VMEM((2,) + tile, f32),
+            pltpu.VMEM((2, 2) + tile, f32),
+            pltpu.VMEM((2, depth, 2) + tile, f32),
+            pltpu.VMEM((events - 2, 2, 1) + tile, f32),
+            pltpu.VMEM((events - 2, 2, depth, 1) + tile, f32),
+            pltpu.VMEM((2, 2 * depth) + tile, f32),
+            pltpu.VMEM((2, 2, 2, levels // 8) + tile, f32),
+            pltpu.VMEM((2, 2, 2, levels // 8) + tile, f32),
+            pltpu.VMEM((2, levels // 8) + tile, f32),
             dma, dma,
             dma((events, 2)), dma((events, 2)),
             dma((events - 1, depth)), dma((events - 1, depth)),
-            dma((2,)), dma((2,)),
+            dma((2,)), dma((2,)), dma((4,)),
+            dma((events - 1, 2, depth)), dma((events - 1, 2, depth)), dma((2, 2)), dma((2, 2)),
         ],
         compiler_params=pltpu.CompilerParams(
-            collective_id=0, has_side_effects=True, vmem_limit_bytes=32 * 1024 * 1024
+            collective_id=0, has_side_effects=True, vmem_limit_bytes=56 * 1024 * 1024
         ),
         cost_estimate=pl.CostEstimate(
             flops=200 * levels * rows * cols, bytes_accessed=22 * levels * rows * cols,

time: 41.7 us -> 35.9 us (0.86)
  Pallas kernels: 35.7 us -> 32.7 us
  local copies, waits for them, and re-layouts: 5.15 us -> 2.36 us
    pallas_call x1, Pallas kernels: 35.7 us -> 32.7 us  [local(): pl.pallas_call(functools.partial(kernel, depth, width), out_shape=(jax.Sh...]
    unnamed x10 -> x4, local copies, waits for them, and re-layouts: 5.15 us -> 2.36 us
where the time goes in v1:
time: 35.9 us; the launch traced here: 35.7 us
  Pallas kernels  32.7 us (91%)
  local copies, waits for them, and re-layouts  2.36 us (7%)
  between operations  0.65 us (2%)
    pallas_call x1, Pallas kernels, local(): pl.pallas_call(functools.partial(kernel, depth, width), out_shape=(jax.Sh...  32.7 us
    unnamed x4, local copies, waits for them, and re-layouts  2.36 us

profile of v1, /device:TPU:1, one launch (start us, length us, event | category | flops | bytes accessed | tf_op | source)
XLA Modules:
  0.0 35.7 jit_solution(10684414807176580785)
XLA Ops:
  0.6 32.7 %shard_map.59 = (f32[64,8,128]{2,1,0:T(8,128)}, f32[32,8,128]{2,1,0:T(8,128)}) custom-call(f32[64,8,128]{2,1,0:T(8,128)} %bitcast.31, f32[64,8,128]{2,1,0:T(8,128)} %bitcast.32, f32[64,8,128]{2,1,0:T(8,128)} %bitcast.33, f32[64,8,128]{2,1,0:T(8,128)} %bitcast.34), custom_call_target="tpu_custom_call" | custom-call | flops 13107200 | bytes 1441792 | tf_op jit(solution)/shard_map/pallas_call | solution.py:607
  33.3 0.0 copy-start
  33.4 1.7 %copy.14 = f32[64,4,256]{2,1,0:T(4,128)} copy(f32[64,4,256]{2,1,0:T(4,128)} %bitcast.30) | data formatting | bytes 524288
  35.1 0.0 copy-done
  35.1 0.7 %copy.15 = f32[32,4,256]{2,1,0:T(4,128)} copy(f32[32,4,256]{2,1,0:T(4,128)S(1)} %bitcast.35) | data formatting | bytes 262144
Async XLA Ops:
  33.3 1.7 %copy-start = (f32[32,8,128]{2,1,0:T(8,128)S(1)}, f32[32,8,128]{2,1,0:T(8,128)}, u32[]{:S(2)}) copy-start(f32[32,8,128]{2,1,0:T(8,128)} %get-tuple-element.5) | copy-start | bytes 393220

commit v2 on v1

--- a/solution.py
+++ b/solution.py
@@ -13,13 +13,13 @@
 
 
 def kernel(
-    depth, width, rhs_hbm, guess_hbm, up_hbm, lat_hbm, out, coarse,
-    rhs, guess, up, lat,
+    depth, width, rhs_hbm, guess_hbm, up_hbm, lat_hbm, out_hbm, coarse_hbm,
+    out, coarse, rhs, guess, up, lat,
     inv, fwd, bwd, first_g, last_g, src, work, res,
     low_in, pack, halo, ends0, ends, coef, edge_out, edge_in,
     row0_out, row0_in, row_out, row_in, row_coef, unit_pack, unit_halo, joined,
     low_send, low_recv, halo_send, halo_recv, end_send, end_recv, edge_send, edge_recv,
-    load_sem, row_send, row_recv, unit_send, unit_recv,
+    load_sem, store_sem, row_send, row_recv, unit_send, unit_recv,
 ):
     levels = rhs_hbm.shape[0]
     rows = 4
@@ -421,7 +421,7 @@
         for peer in peers:
             end_copy(event, buffer, vert, peer).start()
         if event == 0:
-            units_start(0)
+            units_start(1)
 
         def forward(k, carry):
             f_l, f_u = carry
@@ -449,12 +449,13 @@
             return y_l, y_u
 
         lax.fori_loop(1, half, backward, (y_l, y_u), unroll=True)
-        acc = None
-        for t in range(4):
-            acc = packed(acc, work[part(t)], work[part(t + 4)], t, colour)
-        halo_start(event + 1, acc)
-        if event == 0:
-            units_start(1)
+        if event > 0:
+            acc = None
+            for t in range(4):
+                acc = packed(acc, work[part(t)], work[part(t + 4)], t, colour)
+            halo_start(event + 1, acc)
+        if event == 1:
+            units_start(0)
         for peer in peers:
             end_copy(event, buffer, peer, peer).wait_recv()
         if event == 0:
@@ -467,10 +468,18 @@
             from_a = from_a + coef[1, n] * value
         reach[colour] = (from_b, from_a)
         old = guess if event == 0 else out
-        for t in range(8):
-            where = part(t)
-            new = work[where] + first_g[where] * from_b + last_g[where] * from_a
-            out[where] = jnp.where(chosen[None], new, old[where])
+        acc = None
+        for t in range(4):
+            pair = []
+            for where in (part(t), part(t + 4)):
+                new = work[where] + first_g[where] * from_b + last_g[where] * from_a
+                new = jnp.where(chosen[None], new, old[where])
+                out[where] = new
+                pair.append(new)
+            if event == 0:
+                acc = packed(acc, pair[0], pair[1], t, colour)
+        if event == 0:
+            halo_start(1, acc)
         if event == 2 * SWEEPS - 1:
             def keep_source(t, carry):
                 at = pl.ds(pl.multiple_of(t * chunk, chunk), chunk)
@@ -485,17 +494,22 @@
             table = [[row_item(0, e, 2 + i) for i in range(4)] for e in range(depth)]
             mine = [row_item(0, vert, 2 + i) for i in range(6)]
             interface_coefficients(table, mine[:4], mine[4], mine[5], row_coef)
+            halo_wait(1)
+            planes = halo.at[1]
+            continue
         from_b, from_a = zero, zero
         for n in range(2 * depth):
             value = row_item(event, n // 2, n % 2)
             from_b = from_b + row_coef[0, n] * value
             from_a = from_a + row_coef[1, n] * value
-        if event < 2:
+        if event < 3:
             from_sides(lambda side: unit_copy(colour, side).wait_recv())
         halo_wait(event + 1)
         join_planes(event + 1, colour, from_b, from_a)
         planes = joined
 
+    out_store = pltpu.make_async_copy(out, out_hbm, store_sem.at[0])
+    out_store.start()
     from_b = jnp.where(red, reach[0][0], reach[1][0])
     from_a = jnp.where(red, reach[0][1], reach[1][1])
 
@@ -541,6 +555,13 @@
     last = levels // 2 - 1
     lax.fori_loop(1, last, restrict, 0, unroll=True)
 
+    def coarse_store(first, count, i):
+        at = pl.ds(first, count)
+        return pltpu.make_async_copy(coarse.at[at], coarse_hbm.at[at], store_sem.at[i])
+
+    stores = [coarse_store(1, last - 1, 1), coarse_store(0, 1, 2), coarse_store(last, 1, 3)]
+    stores[0].start()
+
     @pl.when(vert > 0)
     def _():
         edge_copy(0).wait_recv()
@@ -551,6 +572,9 @@
 
     coarse[0] = (edge_in[0] + 3.0 * res[0] + 3.0 * res[1] + res[2]) * 0.125
     coarse[last] = (res[top - 2] + 3.0 * res[top - 1] + 3.0 * res[top] + edge_in[1]) * 0.125
+
+    stores[1].start()
+    stores[2].start()
 
     @pl.when(vert < depth - 1)
     def _():
@@ -580,6 +604,9 @@
         @pl.when(ha > 0)
         def _():
             halo_copy(event, 1).wait_send()
+    out_store.wait()
+    for copy in stores:
+        copy.wait()
 
 
 def to_tiles(a):
@@ -603,7 +630,6 @@
     field = pltpu.VMEM((levels,) + tile, f32)
     events = 2 * SWEEPS + 1
     dma = pltpu.SemaphoreType.DMA
-    vmem = pl.BlockSpec(memory_space=pltpu.VMEM)
     smoothed, coarse = pl.pallas_call(
         functools.partial(kernel, depth, width),
         out_shape=(
@@ -611,8 +637,8 @@
             jax.ShapeDtypeStruct((levels // 2,) + tile, f32),
         ),
         in_specs=[pl.BlockSpec(memory_space=pl.ANY)] * 4,
-        out_specs=(vmem, vmem),
-        scratch_shapes=[field] * 12 + [
+        out_specs=(pl.BlockSpec(memory_space=pl.ANY),) * 2,
+        scratch_shapes=[field, pltpu.VMEM((levels // 2,) + tile, f32)] + [field] * 12 + [
             pltpu.VMEM(tile, f32),
             pltpu.VMEM((events, 2, levels // 8) + tile, f32),
             pltpu.VMEM((events, 2, levels // 8) + tile, f32),
@@ -632,7 +658,7 @@
             dma, dma,
             dma((events, 2)), dma((events, 2)),
             dma((events - 1, depth)), dma((events - 1, depth)),
-            dma((2,)), dma((2,)), dma((4,)),
+            dma((2,)), dma((2,)), dma((4,)), dma((4,)),
             dma((events - 1, 2, depth)), dma((events - 1, 2, depth)), dma((2, 2)), dma((2, 2)),
         ],
         compiler_params=pltpu.CompilerParams(

time: 35.9 us -> 35.6 us (level)
  no operation moved by 1% of the time
where the time goes in v2:
time: 35.6 us; the launch traced here: 35.4 us
  Pallas kernels  32.4 us (91%)
  local copies, waits for them, and re-layouts  2.36 us (7%)
  between operations  0.65 us (2%)
    pallas_call x1, Pallas kernels, local(): pl.pallas_call(functools.partial(kernel, depth, width), out_shape=(jax.Sh...  32.4 us
    unnamed x4, local copies, waits for them, and re-layouts  2.36 us

profile of v2, /device:TPU:1, one launch (start us, length us, event | category | flops | bytes accessed | tf_op | source)
XLA Modules:
  0.0 35.4 jit_solution(8588126880385586051)
XLA Ops:
  0.6 32.4 %shard_map.59 = (f32[64,8,128]{2,1,0:T(8,128)}, f32[32,8,128]{2,1,0:T(8,128)}) custom-call(f32[64,8,128]{2,1,0:T(8,128)} %bitcast.31, f32[64,8,128]{2,1,0:T(8,128)} %bitcast.32, f32[64,8,128]{2,1,0:T(8,128)} %bitcast.33, f32[64,8,128]{2,1,0:T(8,128)} %bitcast.34), custom_call_target="tpu_custom_call" | custom-call | flops 13107200 | bytes 1441792 | tf_op jit(solution)/shard_map/pallas_call | solution.py:633
  33.0 0.0 copy-start
  33.0 1.7 %copy.14 = f32[64,4,256]{2,1,0:T(4,128)} copy(f32[64,4,256]{2,1,0:T(4,128)} %bitcast.30) | data formatting | bytes 524288
  34.7 0.0 copy-done
  34.8 0.7 %copy.15 = f32[32,4,256]{2,1,0:T(4,128)} copy(f32[32,4,256]{2,1,0:T(4,128)S(1)} %bitcast.35) | data formatting | bytes 262144
Async XLA Ops:
  33.0 1.7 %copy-start = (f32[32,8,128]{2,1,0:T(8,128)S(1)}, f32[32,8,128]{2,1,0:T(8,128)}, u32[]{:S(2)}) copy-start(f32[32,8,128]{2,1,0:T(8,128)} %get-tuple-element.5) | copy-start | bytes 393220
